TPU v7x, 32 devices: a whole 2x2x4 slice. The times are simulated.
32 devices in a mesh: row: 8 (over z, y), col: 4 (over x, core).
Axes of the slice: x: 2, y: 2, z: 4, core: 2. Of those that a mesh axis runs over, the one named last changes fastest.
Arguments:
- images: float32 [512, 768], P(('row', 'col')), may hold values from -0.21650635 to 0.21650635
- texts: float32 [512, 768], P(('row', 'col')), may hold values from -0.21650635 to 0.21650635
- log_temp: float32 [1], replicated, may hold values from 2 to 2.6
- bias: float32 [1], replicated, may hold values from -7 to -5
Outputs:
- loss: float32 [1], replicated
- d_log_temp: float32 [1], replicated
- d_bias: float32 [1], replicated
- grad_images: float32 [512, 768], P(('row', 'col'))
- grad_texts: float32 [512, 768], P(('row', 'col'))
All inputs are finite; a program needn't handle non-finite values.
Results may differ from a plain program's by a relative error of at most 0.0003.
Values sent between devices are 32-bit elements; how exact they have to be, the bound alone decides.
A program may use at most 64 MiB of HBM per device.

v0:
```python
import jax
import jax.numpy as jnp
from jax import lax
from jax.sharding import PartitionSpec as P


def normalize(x):
    norm = jnp.sqrt(jnp.sum(x * x, axis=1, keepdims=True) + 1e-06)
    return (x / norm, norm)


def unnormalize(unit, norm, grad_unit):
    inner = jnp.sum(unit * grad_unit, axis=1, keepdims=True)
    return (grad_unit - unit * inner) / norm


def tile_terms(img_block, piece, row_idx, col_idx, shard, col_count, temp, shift):
    sim = jnp.dot(
        img_block, piece.T, precision=lax.Precision.HIGHEST, preferred_element_type=jnp.float32
    )
    logit = temp * sim + shift
    img_global = row_idx * (col_count * shard) + jnp.arange(img_block.shape[0], dtype=jnp.int32)
    gathered = jnp.arange(piece.shape[0], dtype=jnp.int32)
    txt_global = (gathered // shard * col_count + col_idx) * shard + gathered % shard
    sign = jnp.where(img_global[:, None] == txt_global[None, :], 1.0, -1.0).astype(jnp.float32)
    pair_grad = -sign * jax.nn.sigmoid(-sign * logit)
    loss_part = jnp.sum(jax.nn.softplus(-sign * logit))
    temp_part = jnp.sum(pair_grad * sim)
    bias_part = jnp.sum(pair_grad)
    return (pair_grad, loss_part, temp_part, bias_part)


def per_device(images, texts, log_temp, bias):
    shard = images.shape[0]
    row_idx = lax.axis_index("row")
    col_idx = lax.axis_index("col")
    col_count = lax.axis_size("col")
    temp = jnp.exp(log_temp[0])
    shift = bias[0]
    unit_img, norm_img = normalize(images)
    unit_txt, norm_txt = normalize(texts)
    img_block = lax.all_gather(unit_img, "col", axis=0, tiled=True)
    txt_block = lax.all_gather(unit_txt, "row", axis=0, tiled=True)
    pair_grad, loss_sum, temp_sum, bias_sum = tile_terms(
        img_block, txt_block, row_idx, col_idx, shard, col_count, temp, shift
    )
    grad_img_part = temp * jnp.dot(
        pair_grad, txt_block, precision=lax.Precision.HIGHEST, preferred_element_type=jnp.float32
    )
    grad_txt_part = temp * lax.dot_general(
        pair_grad,
        img_block,
        (((0,), (0,)), ((), ())),
        precision=lax.Precision.HIGHEST,
        preferred_element_type=jnp.float32,
    )
    grad_unit_txt = lax.psum_scatter(grad_txt_part, "row", scatter_dimension=0, tiled=True)
    grad_unit_img = lax.psum_scatter(grad_img_part, "col", scatter_dimension=0, tiled=True)
    loss_all, temp_all, bias_all = lax.psum((loss_sum, temp_sum, bias_sum), ("row", "col"))
    total_rows = jnp.float32(shard * lax.axis_size("row") * lax.axis_size("col"))
    loss = jnp.reshape(loss_all / total_rows, (1,))
    d_log_temp = jnp.reshape(temp * temp_all / total_rows, (1,))
    d_bias = jnp.reshape(bias_all / total_rows, (1,))
    grad_images = unnormalize(unit_img, norm_img, grad_unit_img)
    grad_texts = unnormalize(unit_txt, norm_txt, grad_unit_txt)
    return (loss, d_log_temp, d_bias, grad_images, grad_texts)


def solution(mesh):
    in_specs = (P(("row", "col"), None), P(("row", "col"), None), P(), P())
    out_specs = (P(), P(), P(), P(("row", "col"), None), P(("row", "col"), None))
    return jax.shard_map(
        per_device, mesh=mesh, in_specs=in_specs, out_specs=out_specs, check_vma=False
    )
```

profile of v0, /device:TPU:0, one launch (start us, length us, event | category | flops | bytes accessed | tf_op | source)
XLA Modules:
  0.0 148.6 jit_solution(17693781503449015708)
XLA Ops:
  7.2 0.0 copy-start.1
  7.2 0.0 reduce-scatter.3.cloned.1.call-start
  8.6 0.9 multiply_reduce_fusion.3
  9.5 0.0 copy-done.1
  9.5 0.1 multiply_reduce_fusion.2
  9.6 0.0 copy-start
  9.7 0.1 broadcast_divide_fusion
  9.7 0.7 copy-done
  10.5 0.1 broadcast_divide_fusion.1
  10.5 6.8 %all_gather.6 = f32[64,768]{1,0:T(8,128)S(1)} all-gather(f32[16,768]{1,0:T(8,128)S(1)} %broadcast_divide_fusion.1), channel_id=1, replica_groups=mesh['row'=8,'col'=4] {'col'}, dimensions={0}, use_global_device_ids=true | all-gather | bytes 245760 | tf_op jit(solution)/shard_map/all_gather | solution.py:42
  17.4 31.7 %all_gather.7 = f32[128,768]{1,0:T(8,128)S(1)} all-gather(f32[16,768]{1,0:T(8,128)S(1)} %broadcast_divide_fusion), channel_id=1, replica_groups=mesh['row'=8,'col'=4] {'row'}, dimensions={0}, use_global_device_ids=true | all-gather | bytes 442368 | tf_op jit(solution)/shard_map/all_gather | solution.py:43
  49.1 1.2 fusion.5
  50.3 1.1 convolution_multiply_fusion.1
  51.3 0.0 reduce-scatter.3.cloned.1.call-update
  51.4 0.0 reduce-scatter.5.cloned.1.call-start
  51.4 1.4 convolution_multiply_fusion
  52.8 0.0 reduce-scatter.5.cloned.1.call-update
  52.8 39.7 %all-reduce = (f32[]{:T(128)}, f32[]{:T(128)}, f32[]{:T(128)}) all-reduce(f32[]{:T(128)} %get-tuple-element.6, f32[]{:T(128)} %get-tuple-element.7, f32[]{:T(128)} %get-tuple-element.5), channel_id=1, replica_groups=mesh['row'=8,'col'=4] {'row','col'}, use_global_device_ids=true, to_apply=%region_3.4 | all-reduce | flops 3 | bytes 24 | tf_op jit(solution)/shard_map/psum | solution.py:59
  94.4 0.0 reduce-scatter.3.cloned.1.call-done
  94.5 0.0 copy-start.2
  94.5 1.1 multiply_reduce_fusion.1
  95.5 0.0 copy-done.2
  95.5 0.7 subtract_divide_fusion.1
  96.2 40.3 %reduce-scatter.5.cloned.1.call-done = f32[16,768]{1,0:T(8,128)} async-done(((f32[128,768]{1,0:T(8,128)}), f32[16,768]{1,0:T(8,128)}) %reduce-scatter.5.cloned.1.call-update) | async-done | bytes 49168 | tf_op jit(solution)/shard_map/reduce_scatter | solution.py:57
  136.6 0.0 copy-start.3
  136.6 1.1 multiply_reduce_fusion
  137.6 0.0 copy-done.3
  137.6 0.7 subtract_divide_fusion
  (4 shorter events, 0.0 us)
Async XLA Ops:
  7.2 2.3 %copy-start.1 = (f32[16,768]{1,0:T(8,128)S(1)}, f32[16,768]{1,0:T(8,128)}, u32[]{:S(2)}) copy-start(f32[16,768]{1,0:T(8,128)} %param.5) | copy-start | bytes 147460
  7.2 87.3 %reduce-scatter.3.cloned.1.call-start = ((), (), s32[]{:S(2)}) async-start(), calls=%async_computation.2 | async-start | bytes 245760 | tf_op jit(solution)/shard_map/reduce_scatter | solution.py:58
  9.6 0.8 copy-start
  51.4 85.2 %reduce-scatter.5.cloned.1.call-start = ((), (), s32[]{:S(2)}) async-start(), calls=%async_computation.3 | async-start | bytes 442368 | tf_op jit(solution)/shard_map/reduce_scatter | solution.py:57
  94.5 1.1 copy-start.2
  136.6 1.1 copy-start.3
Sparse Core Ops, SparseCore 0:
  51.5 20.4 reduce-scatter.2
  75.2 61.3 reduce-scatter.4
where the time goes:
time: 149 us
  blocking collectives  78.3 us (53%)
  waiting for transfers between devices  40.4 us (27%)
  between operations  20.8 us (14%)
  other arithmetic  4.74 us (3%)
  matrix products  3.58 us (2%)
    reduce_scatter x1, waiting for transfers between devices, per_device(): lax.psum_scatter(grad_txt_part, 'row', scatter_dimension=0, tiled=True)  40.3 us
    psum x1, blocking collectives, per_device(): lax.psum((loss_sum, temp_sum, bias_sum), ('row', 'col'))  39.7 us
    all_gather x1, blocking collectives, per_device(): txt_block = lax.all_gather(unit_txt, 'row', axis=0, tiled=True)  31.7 us
    all_gather x1, blocking collectives, per_device(): img_block = lax.all_gather(unit_img, 'col', axis=0, tiled=True)  6.82 us
  transfers between devices with their start and end apart: 2, of which 1 were waited for; matrix products, arithmetic and copies ran while one was open for 2% of the time, Pallas kernels for 0%

commit v1 on v0

v1 whole, which is shorter than its diff:
```python
import functools

import jax
import jax.numpy as jnp
from jax import lax
from jax.experimental import pallas as pl
from jax.experimental.pallas import tpu as pltpu
from jax.sharding import PartitionSpec as P

MESH = pl.DeviceIdType.MESH
BF16 = jnp.bfloat16
F32 = jnp.float32


def split(x):
    hi = x.astype(BF16)
    return hi, (x - hi.astype(F32)).astype(BF16)


def dot(a, b, contract):
    return lax.dot_general(a, b, ((contract[:1], contract[1:]), ((), ())), preferred_element_type=F32)


def normalize(x):
    norm = jnp.sqrt(jnp.sum(x * x, axis=1, keepdims=True) + 1e-06)
    return x / norm, norm


def unnormalize(unit, norm, grad_unit):
    inner = jnp.sum(unit * grad_unit, axis=1, keepdims=True)
    return (grad_unit - unit * inner) / norm


def kernel(
    rows, cols, low,
    log_temp_ref, bias_ref, images_ref, texts_ref,
    grad_img_ref, grad_txt_ref, scalars_ref,
    images_at, texts_at, img_both, txt_both,
    img_all, txt_all, img_part, txt_part, img_recv, txt_recv, sums_img, sums_txt,
    send_img, recv_img, send_txt, recv_txt, send_pimg, recv_pimg, send_ptxt, recv_ptxt,
    send_s1, recv_s1, send_s2, recv_s2, load,
):
    n_img, n_txt = cols * low, rows // low
    shard, width = images_ref.shape
    row, col = lax.axis_index("row"), lax.axis_index("col")
    high, below = lax.div(row, low), lax.rem(row, low)
    g_img = below * cols + col
    g_txt = high

    loads = [
        pltpu.make_async_copy(texts_ref, texts_at, load.at[0]),
        pltpu.make_async_copy(images_ref, images_at, load.at[1]),
    ]
    for item in loads:
        item.start()

    img_peers, txt_peers = [], []
    for step in range(1, n_txt):
        slot = lax.rem(g_txt + step, n_txt)
        txt_peers.append((slot, (slot * low + below, col)))
    for step in range(1, n_img):
        slot = lax.rem(g_img + step, n_img)
        img_peers.append((slot, (high * low + lax.div(slot, cols), lax.rem(slot, cols))))

    barrier = pltpu.get_barrier_semaphore()
    for _, peer in txt_peers + img_peers:
        pl.semaphore_signal(barrier, inc=1, device_id=peer, device_id_type=MESH)

    m_txt, m_img = n_txt * shard, n_img * shard

    def keep(both, slot, offset, x):
        hi, lo = split(x)
        at = pl.multiple_of(slot * shard, shard)
        both[pl.ds(at, shard), :] = hi
        both[pl.ds(offset + at, shard), :] = lo

    loads[0].wait()
    unit_txt, norm_txt = normalize(texts_at[...])
    txt_all[g_txt] = unit_txt
    loads[1].wait()
    unit_img, norm_img = normalize(images_at[...])
    img_all[g_img] = unit_img
    pl.semaphore_wait(barrier, n_img + n_txt - 2)

    def copy(src, dst, send, recv, peer):
        return pltpu.make_async_remote_copy(
            src_ref=src, dst_ref=dst, send_sem=send, recv_sem=recv, device_id=peer, device_id_type=MESH
        )

    def gather(buf, send, recv, me, peers):
        for slot, peer in peers:
            copy(buf.at[me], buf.at[me], send.at[slot], recv.at[me], peer).start()

    def scatter(src, dst, send, recv, me, peers):
        for slot, peer in peers:
            copy(src.at[slot], dst.at[me], send.at[slot], recv.at[me], peer).start()

    def arrive(dst, send, recv, slot, peer):
        copy(dst.at[slot], dst.at[slot], send.at[slot], recv.at[slot], peer).wait_recv()

    def drain(dst, send, recv, peers):
        for slot, peer in peers:
            arrive(dst, send, recv, slot, peer)

    def sent(src, send, recv, peers):
        for slot, peer in peers:
            copy(src.at[slot], src.at[slot], send.at[slot], recv.at[slot], peer).wait_send()

    gather(txt_all, send_txt, recv_txt, g_txt, txt_peers)
    gather(img_all, send_img, recv_img, g_img, img_peers)

    keep(txt_both, g_txt, m_txt, unit_txt)
    keep(img_both, g_img, m_img, unit_img)
    temp = jnp.exp(jnp.full((1, 1), log_temp_ref[0], F32))
    shift = bias_ref[0]
    for slot, peer in img_peers:
        arrive(img_all, send_img, recv_img, slot, peer)
        keep(img_both, slot, m_img, img_all[slot])
    for slot, peer in txt_peers:
        arrive(txt_all, send_txt, recv_txt, slot, peer)
        keep(txt_both, slot, m_txt, txt_all[slot])

    prod = dot(txt_both[...], img_both[...], (1, 1))
    sim = (prod[:m_txt, :m_img] + prod[m_txt:, m_img:]) + (prod[:m_txt, m_img:] + prod[m_txt:, :m_img])
    logit = temp * sim + shift
    at = lax.broadcasted_iota(jnp.int32, (m_txt, m_img), 0) - g_txt * shard
    diagonal = (at == lax.broadcasted_iota(jnp.int32, (m_txt, m_img), 1) - g_img * shard) & (at >= 0) & (at < shard)
    sign = jnp.where(diagonal, 1.0, -1.0).astype(F32)
    margin = -sign * logit
    small = jnp.exp(-jnp.abs(margin))
    pair_grad = -sign * (jnp.where(margin >= 0, 1.0, small) / (1.0 + small))
    soft = jnp.maximum(margin, 0.0) + jnp.log1p(small)

    def total(x):
        return jnp.sum(jnp.sum(x, axis=0, keepdims=True), axis=1, keepdims=True)

    lane = lax.broadcasted_iota(jnp.int32, (8, 128), 1)
    part = jnp.where(lane == 0, total(soft), jnp.where(lane == 1, total(pair_grad * sim), total(pair_grad)))
    sums_img[g_img] = part
    gather(sums_img, send_s1, recv_s1, g_img, img_peers)

    g_hi, g_lo = split(temp * pair_grad)
    g_both = jnp.concatenate([g_hi, g_lo], axis=0)
    pt = dot(jnp.concatenate([g_both, g_both], axis=1), img_both[...], (1, 0))
    txt_part[...] = (pt[:m_txt] + pt[m_txt:]).reshape(n_txt, shard, width)
    scatter(txt_part, txt_recv, send_ptxt, recv_ptxt, g_txt, txt_peers)
    pi = dot(
        jnp.concatenate([g_hi, g_hi, g_lo, g_lo], axis=0),
        jnp.concatenate([txt_both[...], txt_both[...]], axis=0),
        (0, 0),
    )
    img_part[...] = pi.reshape(n_img, shard, width)
    scatter(img_part, img_recv, send_pimg, recv_pimg, g_img, img_peers)

    drain(sums_img, send_s1, recv_s1, img_peers)
    sums_txt[g_txt] = jnp.sum(sums_img[...], axis=0)
    gather(sums_txt, send_s2, recv_s2, g_txt, txt_peers)
    sent(txt_all, send_txt, recv_txt, txt_peers)
    sent(img_all, send_img, recv_img, img_peers)
    sent(sums_img, send_s1, recv_s1, img_peers)

    drain(txt_recv, send_ptxt, recv_ptxt, txt_peers)
    txt_recv[g_txt] = txt_part[g_txt]
    grad_txt_ref[...] = unnormalize(unit_txt, norm_txt, jnp.sum(txt_recv[...], axis=0))
    drain(img_recv, send_pimg, recv_pimg, img_peers)
    img_recv[g_img] = img_part[g_img]
    grad_img_ref[...] = unnormalize(unit_img, norm_img, jnp.sum(img_recv[...], axis=0))

    drain(sums_txt, send_s2, recv_s2, txt_peers)
    count = float(rows * cols * shard)
    final = jnp.sum(sums_txt[...], axis=0) / count
    scalars_ref[...] = jnp.where(lane == 1, temp * final, final)

    sent(txt_part, send_ptxt, recv_ptxt, txt_peers)
    sent(img_part, send_pimg, recv_pimg, img_peers)
    sent(sums_txt, send_s2, recv_s2, txt_peers)


def write_out(grad_img_ref, grad_txt_ref, scalars_ref, loss_ref, d_temp_ref, d_bias_ref, img_ref, txt_ref, sem):
    writes = [
        pltpu.make_async_copy(grad_img_ref, img_ref, sem.at[0]),
        pltpu.make_async_copy(grad_txt_ref, txt_ref, sem.at[1]),
    ]
    for item in writes:
        item.start()
    loss_ref[0] = scalars_ref[0, 0]
    d_temp_ref[0] = scalars_ref[0, 1]
    d_bias_ref[0] = scalars_ref[0, 2]
    for item in writes:
        item.wait()


def per_device(rows, cols, low, images, texts, log_temp, bias):
    shard, width = images.shape
    n_img, n_txt = cols * low, rows // low
    block = (shard, width)
    img_blocks, txt_blocks = pltpu.VMEM((n_img, *block), F32), pltpu.VMEM((n_txt, *block), F32)
    img_sems, txt_sems = pltpu.SemaphoreType.DMA((n_img,)), pltpu.SemaphoreType.DMA((n_txt,))
    vmem, smem = pl.BlockSpec(memory_space=pltpu.VMEM), pl.BlockSpec(memory_space=pltpu.SMEM)
    hbm = pl.BlockSpec(memory_space=pltpu.HBM)
    images, texts = (pltpu.with_memory_space_constraint(x, pltpu.HBM) for x in (images, texts))
    grad_img, grad_txt, scalars = pl.pallas_call(
        functools.partial(kernel, rows, cols, low),
        out_shape=[
            jax.ShapeDtypeStruct(block, F32),
            jax.ShapeDtypeStruct(block, F32),
            jax.ShapeDtypeStruct((8, 128), F32),
        ],
        in_specs=[smem, smem, hbm, hbm],
        out_specs=[vmem, vmem, vmem],
        scratch_shapes=[
            pltpu.VMEM(block, F32), pltpu.VMEM(block, F32),
            pltpu.VMEM((2 * n_img * shard, width), BF16), pltpu.VMEM((2 * n_txt * shard, width), BF16),
            img_blocks, txt_blocks, img_blocks, txt_blocks, img_blocks, txt_blocks,
            pltpu.VMEM((n_img, 8, 128), F32), pltpu.VMEM((n_txt, 8, 128), F32),
            img_sems, img_sems, txt_sems, txt_sems, img_sems, img_sems, txt_sems, txt_sems,
            img_sems, img_sems, txt_sems, txt_sems, pltpu.SemaphoreType.DMA((2,)),
        ],
        compiler_params=pltpu.CompilerParams(
            collective_id=0, has_side_effects=True, vmem_limit_bytes=48 * 1024 * 1024
        ),
        name="sigmoid_loss",
    )(log_temp, bias, images, texts)
    one = jax.ShapeDtypeStruct((1,), F32)
    return pl.pallas_call(
        write_out,
        out_shape=[one, one, one, jax.ShapeDtypeStruct(block, F32), jax.ShapeDtypeStruct(block, F32)],
        in_specs=[vmem, vmem, vmem],
        out_specs=[smem, smem, smem, hbm, hbm],
        scratch_shapes=[pltpu.SemaphoreType.DMA((2,))],
        name="write_out",
    )(grad_img, grad_txt, scalars)


def solution(mesh):
    rows, cols = mesh.shape["row"], mesh.shape["col"]
    low = 1
    while cols * low < rows // low and rows % (2 * low) == 0:
        low *= 2
    in_specs = (P(("row", "col"), None), P(("row", "col"), None), P(), P())
    out_specs = (P(), P(), P(), P(("row", "col"), None), P(("row", "col"), None))
    return jax.shard_map(
        functools.partial(per_device, rows, cols, low),
        mesh=mesh, in_specs=in_specs, out_specs=out_specs, check_vma=False,
    )
```

time: 149 us -> 25.5 us (0.17)
  blocking collectives: 78.3 us -> 0 us
  waiting for transfers between devices: 40.4 us -> 0 us
  Pallas kernels: 0 us -> 21.6 us
  between operations: 20.8 us -> 1.94 us
  other arithmetic: 4.74 us -> 0 us
  matrix products: 3.58 us -> 0 us
    reduce_scatter x2 -> x0, waiting for transfers between devices: 40.3 us -> none  [the longest x1 40.3 us: per_device(): lax.psum_scatter(grad_txt_part, 'row', scatter_dimension=0, tiled=True)]
    psum x1 -> x0, blocking collectives: 39.7 us -> none  [per_device(): lax.psum((loss_sum, temp_sum, bias_sum), ('row', 'col'))]
    all_gather x2 -> x0, blocking collectives: 38.6 us -> none  [the longest x1 31.7 us: per_device(): txt_block = lax.all_gather(unit_txt, 'row', axis=0, tiled=True)]
    pallas_call x0 -> x2, Pallas kernels: none -> 21.6 us  [the longest x1 19.5 us: per_device(): pl.pallas_call(functools.partial(kernel, rows, cols, low), out_shape=[jax...]
    dot_general x3 -> x0, matrix products: 3.58 us -> none  [the longest x1 1.35 us: per_device(): lax.dot_general(pair_grad, img_block, (((0,), (0,)), ((), ())), precision...]
    reduce_sum x4 -> x0, other arithmetic: 3.15 us -> none  [the longest x2 2.11 us: unnormalize(): inner = jnp.sum(unit * grad_unit, axis=1, keepdims=True)]
    div x4 -> x0, other arithmetic: 1.57 us -> none  [the longest x2 1.41 us: unnormalize(): return (grad_unit - unit * inner) / norm]
  transfers between devices with their start and end apart: 2 -> 0, of which waited for: 1 -> 0; matrix products, arithmetic and copies ran while one was open for 2% -> 0% of each run, Pallas kernels for 0% -> 0%
where the time goes in v1:
time: 25.5 us; the launch traced here: 25.3 us
  Pallas kernels  21.6 us (85%)
  between operations  1.94 us (8%)
  local copies, waits for them, and re-layouts  1.8 us (7%)
    pallas_call x1, Pallas kernels, per_device(): pl.pallas_call(functools.partial(kernel, rows, cols, low), out_shape=[jax...  19.5 us
    pallas_call x1, Pallas kernels, per_device(): pl.pallas_call(write_out, out_shape=[one, one, one, jax.ShapeDtypeStruct(...  2.01 us
    unnamed x6, local copies, waits for them, and re-layouts  1.8 us

profile of v1, /device:TPU:0, one launch (start us, length us, event | category | flops | bytes accessed | tf_op | source)
XLA Modules:
  0.0 25.3 jit_solution(14185110704359425618)
XLA Ops:
  1.9 19.5 %sigmoid_loss.1 = (f32[16,768]{1,0:T(8,128)S(1)}, f32[16,768]{1,0:T(8,128)S(1)}, f32[8,128]{1,0:T(8,128)S(1)}) custom-call(f32[1]{0:T(128)S(6)} %copy.9.log_temp_ref, f32[1]{0:T(128)S(6)} %copy.10.bias_ref, f32[16,768]{1,0:T(8,128)} %images_ref.1, f32[16,768]{1,0:T(8,128)} %texts_ref.1), custom_call_target="tpu_custom_call" | custom-call | tf_op jit(solution)/shard_map/sigmoid_loss/pallas_call | solution.py:202
  21.5 0.0 copy-start
  21.5 0.6 %copy-done = f32[16,768]{1,0:T(8,128)} copy-done((f32[16,768]{1,0:T(8,128)}, f32[16,768]{1,0:T(8,128)S(1)}, u32[]{:S(2)}) %copy-start) | copy-done | bytes 49176
  22.1 0.0 copy-start.1
  22.1 0.6 %copy-done.1 = f32[16,768]{1,0:T(8,128)} copy-done((f32[16,768]{1,0:T(8,128)}, f32[16,768]{1,0:T(8,128)S(1)}, u32[]{:S(2)}) %copy-start.1) | copy-done | bytes 49176
  22.7 0.0 copy-start.2
  22.7 0.6 %copy-done.2 = f32[8,128]{1,0:T(8,128)} copy-done((f32[8,128]{1,0:T(8,128)}, f32[8,128]{1,0:T(8,128)S(1)}, u32[]{:S(2)}) %copy-start.2) | copy-done | bytes 4120
  23.3 2.0 %write_out.1 = (f32[1]{0:T(128)}, f32[1]{0:T(128)}, f32[1]{0:T(128)}, f32[16,768]{1,0:T(8,128)}, f32[16,768]{1,0:T(8,128)}) custom-call(f32[16,768]{1,0:T(8,128)} %copy-done, f32[16,768]{1,0:T(8,128)} %copy-done.1, f32[8,128]{1,0:T(8,128)} %copy-done.2), custom_call_target="tpu_custom_call" | custom-call | tf_op jit(solution)/shard_map/write_out/pallas_call | solution.py:225
Async XLA Ops:
  21.5 0.6 %copy-start = (f32[16,768]{1,0:T(8,128)}, f32[16,768]{1,0:T(8,128)S(1)}, u32[]{:S(2)}) copy-start(f32[16,768]{1,0:T(8,128)S(1)} %get-tuple-element.8.grad_img_ref) | copy-start | bytes 147460
  22.1 0.6 %copy-start.1 = (f32[16,768]{1,0:T(8,128)}, f32[16,768]{1,0:T(8,128)S(1)}, u32[]{:S(2)}) copy-start(f32[16,768]{1,0:T(8,128)S(1)} %get-tuple-element.9.grad_txt_ref) | copy-start | bytes 147460
  22.7 0.6 %copy-start.2 = (f32[8,128]{1,0:T(8,128)}, f32[8,128]{1,0:T(8,128)S(1)}, u32[]{:S(2)}) copy-start(f32[8,128]{1,0:T(8,128)S(1)} %get-tuple-element.10.scalars_ref) | copy-start | bytes 12292

commit v2 on v1

--- a/solution.py
+++ b/solution.py
@@ -129,21 +129,22 @@
     margin = -sign * logit
     small = jnp.exp(-jnp.abs(margin))
     pair_grad = -sign * (jnp.where(margin >= 0, 1.0, small) / (1.0 + small))
-    soft = jnp.maximum(margin, 0.0) + jnp.log1p(small)
 
     def total(x):
         return jnp.sum(jnp.sum(x, axis=0, keepdims=True), axis=1, keepdims=True)
-
-    lane = lax.broadcasted_iota(jnp.int32, (8, 128), 1)
-    part = jnp.where(lane == 0, total(soft), jnp.where(lane == 1, total(pair_grad * sim), total(pair_grad)))
-    sums_img[g_img] = part
-    gather(sums_img, send_s1, recv_s1, g_img, img_peers)
 
     g_hi, g_lo = split(temp * pair_grad)
     g_both = jnp.concatenate([g_hi, g_lo], axis=0)
     pt = dot(jnp.concatenate([g_both, g_both], axis=1), img_both[...], (1, 0))
     txt_part[...] = (pt[:m_txt] + pt[m_txt:]).reshape(n_txt, shard, width)
     scatter(txt_part, txt_recv, send_ptxt, recv_ptxt, g_txt, txt_peers)
+
+    soft = jnp.maximum(margin, 0.0) + jnp.log1p(small)
+    lane = lax.broadcasted_iota(jnp.int32, (8, 128), 1)
+    part = jnp.where(lane == 0, total(soft), jnp.where(lane == 1, total(pair_grad * sim), total(pair_grad)))
+    sums_img[g_img] = part
+    gather(sums_img, send_s1, recv_s1, g_img, img_peers)
+
     pi = dot(
         jnp.concatenate([g_hi, g_hi, g_lo, g_lo], axis=0),
         jnp.concatenate([txt_both[...], txt_both[...]], axis=0),
@@ -159,12 +160,16 @@
     sent(img_all, send_img, recv_img, img_peers)
     sent(sums_img, send_s1, recv_s1, img_peers)
 
-    drain(txt_recv, send_ptxt, recv_ptxt, txt_peers)
-    txt_recv[g_txt] = txt_part[g_txt]
-    grad_txt_ref[...] = unnormalize(unit_txt, norm_txt, jnp.sum(txt_recv[...], axis=0))
-    drain(img_recv, send_pimg, recv_pimg, img_peers)
-    img_recv[g_img] = img_part[g_img]
-    grad_img_ref[...] = unnormalize(unit_img, norm_img, jnp.sum(img_recv[...], axis=0))
+    grad_txt = txt_part[g_txt]
+    for slot, peer in txt_peers:
+        arrive(txt_recv, send_ptxt, recv_ptxt, slot, peer)
+        grad_txt = grad_txt + txt_recv[slot]
+    grad_txt_ref[...] = unnormalize(unit_txt, norm_txt, grad_txt)
+    grad_img = img_part[g_img]
+    for slot, peer in img_peers:
+        arrive(img_recv, send_pimg, recv_pimg, slot, peer)
+        grad_img = grad_img + img_recv[slot]
+    grad_img_ref[...] = unnormalize(unit_img, norm_img, grad_img)
 
     drain(sums_txt, send_s2, recv_s2, txt_peers)
     count = float(rows * cols * shard)
@@ -176,16 +181,16 @@
     sent(sums_txt, send_s2, recv_s2, txt_peers)
 
 
-def write_out(grad_img_ref, grad_txt_ref, scalars_ref, loss_ref, d_temp_ref, d_bias_ref, img_ref, txt_ref, sem):
+def write_out(grad_img_ref, grad_txt_ref, scalars_ref, loss_ref, d_temp_ref, d_bias_ref, img_ref, txt_ref, parts, sem):
     writes = [
         pltpu.make_async_copy(grad_img_ref, img_ref, sem.at[0]),
         pltpu.make_async_copy(grad_txt_ref, txt_ref, sem.at[1]),
     ]
+    for at, ref in enumerate((loss_ref, d_temp_ref, d_bias_ref)):
+        parts[at] = scalars_ref[0:1, at : at + 1]
+        writes.append(pltpu.make_async_copy(parts.at[at], ref, sem.at[2 + at]))
     for item in writes:
         item.start()
-    loss_ref[0] = scalars_ref[0, 0]
-    d_temp_ref[0] = scalars_ref[0, 1]
-    d_bias_ref[0] = scalars_ref[0, 2]
     for item in writes:
         item.wait()
 
@@ -202,9 +207,9 @@
     grad_img, grad_txt, scalars = pl.pallas_call(
         functools.partial(kernel, rows, cols, low),
         out_shape=[
-            jax.ShapeDtypeStruct(block, F32),
-            jax.ShapeDtypeStruct(block, F32),
-            jax.ShapeDtypeStruct((8, 128), F32),
+            pltpu.VMEM(block, F32),
+            pltpu.VMEM(block, F32),
+            pltpu.VMEM((8, 128), F32),
         ],
         in_specs=[smem, smem, hbm, hbm],
         out_specs=[vmem, vmem, vmem],
@@ -221,15 +226,17 @@
         ),
         name="sigmoid_loss",
     )(log_temp, bias, images, texts)
-    one = jax.ShapeDtypeStruct((1,), F32)
-    return pl.pallas_call(
+    one = jax.ShapeDtypeStruct((1, 1), F32)
+    held = (pltpu.with_memory_space_constraint(x, pltpu.VMEM) for x in (grad_img, grad_txt, scalars))
+    loss, d_temp, d_bias, grad_img, grad_txt = pl.pallas_call(
         write_out,
         out_shape=[one, one, one, jax.ShapeDtypeStruct(block, F32), jax.ShapeDtypeStruct(block, F32)],
         in_specs=[vmem, vmem, vmem],
-        out_specs=[smem, smem, smem, hbm, hbm],
-        scratch_shapes=[pltpu.SemaphoreType.DMA((2,))],
+        out_specs=[hbm] * 5,
+        scratch_shapes=[pltpu.VMEM((3, 1, 1), F32), pltpu.SemaphoreType.DMA((5,))],
         name="write_out",
-    )(grad_img, grad_txt, scalars)
+    )(*held)
+    return loss.reshape(1), d_temp.reshape(1), d_bias.reshape(1), grad_img, grad_txt
 
 
 def solution(mesh):

time: 25.5 us -> 22.5 us (0.88)
  local copies, waits for them, and re-layouts: 1.8 us -> 0 us
  Pallas kernels: 21.6 us -> 20.4 us
    unnamed x6 -> x0, local copies, waits for them, and re-layouts: 1.8 us -> none
    pallas_call x1, Pallas kernels: 2.01 us -> 0.69 us  [per_device(): pl.pallas_call(write_out, out_shape=[one, one, one, jax.ShapeDtypeStruct(...]
where the time goes in v2:
time: 22.5 us; the launch traced here: 22.3 us
  Pallas kernels  20.4 us (91%)
  between operations  1.93 us (9%)
    pallas_call x1, Pallas kernels, per_device(): pl.pallas_call(functools.partial(kernel, rows, cols, low), out_shape=[plt...  19.7 us
    pallas_call x1, Pallas kernels, per_device(): pl.pallas_call(write_out, out_shape=[one, one, one, jax.ShapeDtypeStruct(...  0.69 us

profile of v2, /device:TPU:0, one launch (start us, length us, event | category | flops | bytes accessed | tf_op | source)
XLA Modules:
  0.0 22.3 jit_solution(10380682724651555517)
XLA Ops:
  1.9 19.7 %sigmoid_loss.1 = (f32[16,768]{1,0:T(8,128)S(1)}, f32[16,768]{1,0:T(8,128)S(1)}, f32[8,128]{1,0:T(8,128)S(1)}) custom-call(f32[1]{0:T(128)S(6)} %copy.9.log_temp_ref, f32[1]{0:T(128)S(6)} %copy.10.bias_ref, f32[16,768]{1,0:T(8,128)} %images_ref.1, f32[16,768]{1,0:T(8,128)} %texts_ref.1), custom_call_target="tpu_custom_call" | custom-call | tf_op jit(solution)/shard_map/sigmoid_loss/pallas_call | solution.py:207
  21.6 0.7 %write_out.1 = (f32[1,1]{1,0:T(1,128)}, f32[1,1]{1,0:T(1,128)}, f32[1,1]{1,0:T(1,128)}, f32[16,768]{1,0:T(8,128)}, f32[16,768]{1,0:T(8,128)}) custom-call(f32[16,768]{1,0:T(8,128)S(1)} %get-tuple-element.13.grad_img_ref, f32[16,768]{1,0:T(8,128)S(1)} %get-tuple-element.14.grad_txt_ref, f32[8,128]{1,0:T(8,128)S(1)} %get-tuple-element.15.scalars_ref), custom_call_target="tpu_custom_call" | custom-call | tf_op jit(solution)/shard_map/write_out/pallas_call | solution.py:231

commit v3 on v2

--- a/solution.py
+++ b/solution.py
@@ -21,6 +21,17 @@
     return lax.dot_general(a, b, ((contract[:1], contract[1:]), ((), ())), preferred_element_type=F32)
 
 
+def paired(slot, step, count):
+    if count & (count - 1):
+        return lax.rem(slot + step, count)
+    bit = 1
+    while bit < count:
+        if step & bit:
+            slot = slot + bit - 2 * bit * lax.rem(lax.div(slot, bit), 2)
+        bit *= 2
+    return slot
+
+
 def normalize(x):
     norm = jnp.sqrt(jnp.sum(x * x, axis=1, keepdims=True) + 1e-06)
     return x / norm, norm
@@ -33,9 +44,9 @@
 
 def kernel(
     rows, cols, low,
-    log_temp_ref, bias_ref, images_ref, texts_ref,
+    scale_ref, images_ref, texts_ref,
     grad_img_ref, grad_txt_ref, scalars_ref,
-    images_at, texts_at, img_both, txt_both,
+    images_at, texts_at, img_both,
     img_all, txt_all, img_part, txt_part, img_recv, txt_recv, sums_img, sums_txt,
     send_img, recv_img, send_txt, recv_txt, send_pimg, recv_pimg, send_ptxt, recv_ptxt,
     send_s1, recv_s1, send_s2, recv_s2, load,
@@ -56,17 +67,25 @@
 
     img_peers, txt_peers = [], []
     for step in range(1, n_txt):
-        slot = lax.rem(g_txt + step, n_txt)
+        slot = paired(g_txt, step, n_txt)
         txt_peers.append((slot, (slot * low + below, col)))
+    def img_device(slot):
+        return high * low + lax.div(slot, cols), lax.rem(slot, cols)
+
+    def sibling(slot):
+        return slot + 1 - 2 * lax.rem(slot, 2)
+
     for step in range(1, n_img):
-        slot = lax.rem(g_img + step, n_img)
-        img_peers.append((slot, (high * low + lax.div(slot, cols), lax.rem(slot, cols))))
+        slot = 2 * paired(lax.div(g_img, 2), step // 2, n_img // 2) + lax.rem(g_img + step, 2)
+        img_peers.append((slot, img_device(slot)))
+    same_core, other_core = img_peers[1::2], img_peers[0::2]
+    twin = other_core[0]
 
     barrier = pltpu.get_barrier_semaphore()
     for _, peer in txt_peers + img_peers:
         pl.semaphore_signal(barrier, inc=1, device_id=peer, device_id_type=MESH)
 
-    m_txt, m_img = n_txt * shard, n_img * shard
+    m_img = n_img * shard
 
     def keep(both, slot, offset, x):
         hi, lo = split(x)
@@ -107,51 +126,63 @@
             copy(src.at[slot], src.at[slot], send.at[slot], recv.at[slot], peer).wait_send()
 
     gather(txt_all, send_txt, recv_txt, g_txt, txt_peers)
-    gather(img_all, send_img, recv_img, g_img, img_peers)
-
-    keep(txt_both, g_txt, m_txt, unit_txt)
+    gather(img_all, send_img, recv_img, g_img, [twin] + same_core)
+
     keep(img_both, g_img, m_img, unit_img)
-    temp = jnp.exp(jnp.full((1, 1), log_temp_ref[0], F32))
-    shift = bias_ref[0]
-    for slot, peer in img_peers:
+    for slot, peer in same_core:
+        arrive(img_all, send_img, recv_img, slot, peer)
+        copy(img_all.at[slot], img_all.at[slot], send_img.at[sibling(slot)], recv_img.at[slot], twin[1]).start()
+        keep(img_both, slot, m_img, img_all[slot])
+    for slot, peer in other_core:
         arrive(img_all, send_img, recv_img, slot, peer)
         keep(img_both, slot, m_img, img_all[slot])
+
+    def total(x):
+        return jnp.sum(jnp.sum(x, axis=0, keepdims=True), axis=1, keepdims=True)
+
+    def fold(x):
+        return sum(
+            x[r : r + 8, c : c + 128] for r in range(0, x.shape[0], 8) for c in range(0, x.shape[1], 128)
+        )
+
+    temp = jnp.exp(scale_ref[:, 0:1])
+    shift = scale_ref[:, 1:2]
+    his, los = ([part] for part in split(unit_txt))
     for slot, peer in txt_peers:
         arrive(txt_all, send_txt, recv_txt, slot, peer)
-        keep(txt_both, slot, m_txt, txt_all[slot])
-
-    prod = dot(txt_both[...], img_both[...], (1, 1))
-    sim = (prod[:m_txt, :m_img] + prod[m_txt:, m_img:]) + (prod[:m_txt, m_img:] + prod[m_txt:, :m_img])
+        hi, lo = split(txt_all[slot])
+        his.append(hi)
+        los.append(lo)
+    m_txt = n_txt * shard
+    txt_both = jnp.concatenate(his + los, axis=0)
+    prod = dot(txt_both, img_both[...], (1, 1))
+    near, far = prod[:m_txt], prod[m_txt:]
+    sim = (near[:, :m_img] + far[:, m_img:]) + (near[:, m_img:] + far[:, :m_img])
     logit = temp * sim + shift
-    at = lax.broadcasted_iota(jnp.int32, (m_txt, m_img), 0) - g_txt * shard
-    diagonal = (at == lax.broadcasted_iota(jnp.int32, (m_txt, m_img), 1) - g_img * shard) & (at >= 0) & (at < shard)
-    sign = jnp.where(diagonal, 1.0, -1.0).astype(F32)
+    at = lax.broadcasted_iota(jnp.int32, (m_txt, m_img), 0)
+    match = at == lax.broadcasted_iota(jnp.int32, (m_txt, m_img), 1) - g_img * shard
+    sign = jnp.where(match & (at < shard), 1.0, -1.0).astype(F32)
     margin = -sign * logit
     small = jnp.exp(-jnp.abs(margin))
     pair_grad = -sign * (jnp.where(margin >= 0, 1.0, small) / (1.0 + small))
-
-    def total(x):
-        return jnp.sum(jnp.sum(x, axis=0, keepdims=True), axis=1, keepdims=True)
-
     g_hi, g_lo = split(temp * pair_grad)
     g_both = jnp.concatenate([g_hi, g_lo], axis=0)
     pt = dot(jnp.concatenate([g_both, g_both], axis=1), img_both[...], (1, 0))
-    txt_part[...] = (pt[:m_txt] + pt[m_txt:]).reshape(n_txt, shard, width)
-    scatter(txt_part, txt_recv, send_ptxt, recv_ptxt, g_txt, txt_peers)
-
-    soft = jnp.maximum(margin, 0.0) + jnp.log1p(small)
-    lane = lax.broadcasted_iota(jnp.int32, (8, 128), 1)
-    part = jnp.where(lane == 0, total(soft), jnp.where(lane == 1, total(pair_grad * sim), total(pair_grad)))
-    sums_img[g_img] = part
+    pt = pt[:m_txt] + pt[m_txt:]
+    for at, slot in enumerate([g_txt] + [slot for slot, _ in txt_peers]):
+        txt_part[slot] = pt[at * shard : (at + 1) * shard]
+    scatter(txt_part, txt_recv, send_ptxt, recv_ptxt, g_txt, txt_peers[::-1])
+
+    terms = (jnp.maximum(margin, 0.0) + jnp.log1p(small), pair_grad * sim, pair_grad)
+    sums_img[g_img] = jnp.concatenate([fold(x) for x in terms], axis=0)
     gather(sums_img, send_s1, recv_s1, g_img, img_peers)
-
     pi = dot(
         jnp.concatenate([g_hi, g_hi, g_lo, g_lo], axis=0),
-        jnp.concatenate([txt_both[...], txt_both[...]], axis=0),
+        jnp.concatenate([txt_both, txt_both], axis=0),
         (0, 0),
     )
     img_part[...] = pi.reshape(n_img, shard, width)
-    scatter(img_part, img_recv, send_pimg, recv_pimg, g_img, img_peers)
+    scatter(img_part, img_recv, send_pimg, recv_pimg, g_img, img_peers[::-1])
 
     drain(sums_img, send_s1, recv_s1, img_peers)
     sums_txt[g_txt] = jnp.sum(sums_img[...], axis=0)
@@ -174,7 +205,9 @@
     drain(sums_txt, send_s2, recv_s2, txt_peers)
     count = float(rows * cols * shard)
     final = jnp.sum(sums_txt[...], axis=0) / count
-    scalars_ref[...] = jnp.where(lane == 1, temp * final, final)
+    loss, d_temp, d_bias = (total(final[at : at + 8]) for at in (0, 8, 16))
+    lane = lax.broadcasted_iota(jnp.int32, (8, 128), 1)
+    scalars_ref[...] = jnp.where(lane == 0, loss, jnp.where(lane == 1, temp * d_temp, d_bias))
 
     sent(txt_part, send_ptxt, recv_ptxt, txt_peers)
     sent(img_part, send_pimg, recv_pimg, img_peers)
@@ -201,9 +234,9 @@
     block = (shard, width)
     img_blocks, txt_blocks = pltpu.VMEM((n_img, *block), F32), pltpu.VMEM((n_txt, *block), F32)
     img_sems, txt_sems = pltpu.SemaphoreType.DMA((n_img,)), pltpu.SemaphoreType.DMA((n_txt,))
-    vmem, smem = pl.BlockSpec(memory_space=pltpu.VMEM), pl.BlockSpec(memory_space=pltpu.SMEM)
-    hbm = pl.BlockSpec(memory_space=pltpu.HBM)
+    vmem, hbm = pl.BlockSpec(memory_space=pltpu.VMEM), pl.BlockSpec(memory_space=pltpu.HBM)
     images, texts = (pltpu.with_memory_space_constraint(x, pltpu.HBM) for x in (images, texts))
+    both = jnp.where(lax.broadcasted_iota(jnp.int32, (1, 128), 1) == 0, log_temp[0], bias[0])
     grad_img, grad_txt, scalars = pl.pallas_call(
         functools.partial(kernel, rows, cols, low),
         out_shape=[
@@ -211,13 +244,13 @@
             pltpu.VMEM(block, F32),
             pltpu.VMEM((8, 128), F32),
         ],
-        in_specs=[smem, smem, hbm, hbm],
+        in_specs=[vmem, hbm, hbm],
         out_specs=[vmem, vmem, vmem],
         scratch_shapes=[
             pltpu.VMEM(block, F32), pltpu.VMEM(block, F32),
-            pltpu.VMEM((2 * n_img * shard, width), BF16), pltpu.VMEM((2 * n_txt * shard, width), BF16),
+            pltpu.VMEM((2 * n_img * shard, width), BF16),
             img_blocks, txt_blocks, img_blocks, txt_blocks, img_blocks, txt_blocks,
-            pltpu.VMEM((n_img, 8, 128), F32), pltpu.VMEM((n_txt, 8, 128), F32),
+            pltpu.VMEM((n_img, 24, 128), F32), pltpu.VMEM((n_txt, 24, 128), F32),
             img_sems, img_sems, txt_sems, txt_sems, img_sems, img_sems, txt_sems, txt_sems,
             img_sems, img_sems, txt_sems, txt_sems, pltpu.SemaphoreType.DMA((2,)),
         ],
@@ -225,7 +258,7 @@
             collective_id=0, has_side_effects=True, vmem_limit_bytes=48 * 1024 * 1024
         ),
         name="sigmoid_loss",
-    )(log_temp, bias, images, texts)
+    )(both, images, texts)
     one = jax.ShapeDtypeStruct((1, 1), F32)
     held = (pltpu.with_memory_space_constraint(x, pltpu.VMEM) for x in (grad_img, grad_txt, scalars))
     loss, d_temp, d_bias, grad_img, grad_txt = pl.pallas_call(

time: 22.5 us -> 23.6 us (1.049)
  Pallas kernels: 20.4 us -> 21.5 us
    pallas_call x1, Pallas kernels: 19.7 us -> 20.8 us  [per_device(): pl.pallas_call(functools.partial(kernel, rows, cols, low), out_shape=[plt...]
where the time goes in v3:
time: 23.6 us; the launch traced here: 23.4 us
  Pallas kernels  21.5 us (91%)
  between operations  1.94 us (8%)
    pallas_call x1, Pallas kernels, per_device(): pl.pallas_call(functools.partial(kernel, rows, cols, low), out_shape=[plt...  20.8 us
    pallas_call x1, Pallas kernels, per_device(): pl.pallas_call(write_out, out_shape=[one, one, one, jax.ShapeDtypeStruct(...  0.69 us

profile of v3, /device:TPU:0, one launch (start us, length us, event | category | flops | bytes accessed | tf_op | source)
XLA Modules:
  0.0 23.4 jit_solution(206383035796678026)
XLA Ops:
  1.9 20.8 %sigmoid_loss.1 = (f32[16,768]{1,0:T(8,128)S(1)}, f32[16,768]{1,0:T(8,128)S(1)}, f32[8,128]{1,0:T(8,128)S(1)}) custom-call(f32[1,128]{1,0:T(1,128)S(1)} %compare_select_fusion.scale_ref, f32[16,768]{1,0:T(8,128)} %images_ref.1, f32[16,768]{1,0:T(8,128)} %texts_ref.1), custom_call_target="tpu_custom_call" | custom-call | tf_op jit(solution)/shard_map/sigmoid_loss/pallas_call | solution.py:240
  22.7 0.7 %write_out.1 = (f32[1,1]{1,0:T(1,128)}, f32[1,1]{1,0:T(1,128)}, f32[1,1]{1,0:T(1,128)}, f32[16,768]{1,0:T(8,128)}, f32[16,768]{1,0:T(8,128)}) custom-call(f32[16,768]{1,0:T(8,128)S(1)} %get-tuple-element.13.grad_img_ref, f32[16,768]{1,0:T(8,128)S(1)} %get-tuple-element.14.grad_txt_ref, f32[8,128]{1,0:T(8,128)S(1)} %get-tuple-element.15.scalars_ref), custom_call_target="tpu_custom_call" | custom-call | tf_op jit(solution)/shard_map/write_out/pallas_call | solution.py:264
  (1 shorter events, 0.0 us)

commit v4 on v3

--- a/solution.py
+++ b/solution.py
@@ -72,14 +72,9 @@
     def img_device(slot):
         return high * low + lax.div(slot, cols), lax.rem(slot, cols)
 
-    def sibling(slot):
-        return slot + 1 - 2 * lax.rem(slot, 2)
-
     for step in range(1, n_img):
         slot = 2 * paired(lax.div(g_img, 2), step // 2, n_img // 2) + lax.rem(g_img + step, 2)
         img_peers.append((slot, img_device(slot)))
-    same_core, other_core = img_peers[1::2], img_peers[0::2]
-    twin = other_core[0]
 
     barrier = pltpu.get_barrier_semaphore()
     for _, peer in txt_peers + img_peers:
@@ -126,63 +121,67 @@
             copy(src.at[slot], src.at[slot], send.at[slot], recv.at[slot], peer).wait_send()
 
     gather(txt_all, send_txt, recv_txt, g_txt, txt_peers)
-    gather(img_all, send_img, recv_img, g_img, [twin] + same_core)
+    gather(img_all, send_img, recv_img, g_img, img_peers)
 
     keep(img_both, g_img, m_img, unit_img)
-    for slot, peer in same_core:
-        arrive(img_all, send_img, recv_img, slot, peer)
-        copy(img_all.at[slot], img_all.at[slot], send_img.at[sibling(slot)], recv_img.at[slot], twin[1]).start()
-        keep(img_both, slot, m_img, img_all[slot])
-    for slot, peer in other_core:
+    for slot, peer in img_peers:
         arrive(img_all, send_img, recv_img, slot, peer)
         keep(img_both, slot, m_img, img_all[slot])
 
     def total(x):
         return jnp.sum(jnp.sum(x, axis=0, keepdims=True), axis=1, keepdims=True)
 
-    def fold(x):
-        return sum(
-            x[r : r + 8, c : c + 128] for r in range(0, x.shape[0], 8) for c in range(0, x.shape[1], 128)
-        )
-
     temp = jnp.exp(scale_ref[:, 0:1])
     shift = scale_ref[:, 1:2]
-    his, los = ([part] for part in split(unit_txt))
-    for slot, peer in txt_peers:
-        arrive(txt_all, send_txt, recv_txt, slot, peer)
-        hi, lo = split(txt_all[slot])
-        his.append(hi)
-        los.append(lo)
-    m_txt = n_txt * shard
-    txt_both = jnp.concatenate(his + los, axis=0)
-    prod = dot(txt_both, img_both[...], (1, 1))
-    near, far = prod[:m_txt], prod[m_txt:]
-    sim = (near[:, :m_img] + far[:, m_img:]) + (near[:, m_img:] + far[:, :m_img])
-    logit = temp * sim + shift
-    at = lax.broadcasted_iota(jnp.int32, (m_txt, m_img), 0)
-    match = at == lax.broadcasted_iota(jnp.int32, (m_txt, m_img), 1) - g_img * shard
-    sign = jnp.where(match & (at < shard), 1.0, -1.0).astype(F32)
-    margin = -sign * logit
-    small = jnp.exp(-jnp.abs(margin))
-    pair_grad = -sign * (jnp.where(margin >= 0, 1.0, small) / (1.0 + small))
-    g_hi, g_lo = split(temp * pair_grad)
-    g_both = jnp.concatenate([g_hi, g_lo], axis=0)
-    pt = dot(jnp.concatenate([g_both, g_both], axis=1), img_both[...], (1, 0))
-    pt = pt[:m_txt] + pt[m_txt:]
-    for at, slot in enumerate([g_txt] + [slot for slot, _ in txt_peers]):
-        txt_part[slot] = pt[at * shard : (at + 1) * shard]
-    scatter(txt_part, txt_recv, send_ptxt, recv_ptxt, g_txt, txt_peers[::-1])
-
-    terms = (jnp.maximum(margin, 0.0) + jnp.log1p(small), pair_grad * sim, pair_grad)
-    sums_img[g_img] = jnp.concatenate([fold(x) for x in terms], axis=0)
+    order = [(g_txt, None)] + txt_peers
+    half = max(1, n_txt // 2)
+    his, los, grads_hi, grads_lo = [], [], [], []
+    loss_sum = temp_sum = bias_sum = 0.0
+    for first in range(0, n_txt, half):
+        group = order[first : first + half]
+        rows_here = len(group) * shard
+        for slot, peer in group:
+            if peer is not None:
+                arrive(txt_all, send_txt, recv_txt, slot, peer)
+        txt_hi, txt_lo = split(jnp.concatenate([txt_all[slot] for slot, _ in group], axis=0))
+        prod = dot(jnp.concatenate([txt_hi, txt_lo], axis=0), img_both[...], (1, 1))
+        near, far = prod[:rows_here], prod[rows_here:]
+        sim = (near[:, :m_img] + far[:, m_img:]) + (near[:, m_img:] + far[:, :m_img])
+        logit = temp * sim + shift
+        sign = -1.0
+        if first == 0:
+            at = lax.broadcasted_iota(jnp.int32, (rows_here, m_img), 0)
+            match = at == lax.broadcasted_iota(jnp.int32, (rows_here, m_img), 1) - g_img * shard
+            sign = jnp.where(match & (at < shard), 1.0, -1.0).astype(F32)
+        margin = -sign * logit
+        small = jnp.exp(-jnp.abs(margin))
+        pair_grad = -sign * (jnp.where(margin >= 0, 1.0, small) / (1.0 + small))
+        g_hi, g_lo = split(temp * pair_grad)
+        g_both = jnp.concatenate([g_hi, g_lo], axis=0)
+        pt = dot(jnp.concatenate([g_both, g_both], axis=1), img_both[...], (1, 0))
+        pt = pt[:rows_here] + pt[rows_here:]
+        for at, (slot, peer) in enumerate(group):
+            txt_part[slot] = pt[at * shard : (at + 1) * shard]
+        scatter(txt_part, txt_recv, send_ptxt, recv_ptxt, g_txt, [item for item in group if item[1] is not None])
+        loss_sum += total(jnp.maximum(margin, 0.0) + jnp.log1p(small))
+        temp_sum += total(pair_grad * sim)
+        bias_sum += total(pair_grad)
+        his.append(txt_hi)
+        los.append(txt_lo)
+        grads_hi.append(g_hi)
+        grads_lo.append(g_lo)
+
+    lane = lax.broadcasted_iota(jnp.int32, (8, 128), 1)
+    part = jnp.where(lane == 0, loss_sum, jnp.where(lane == 1, temp_sum, bias_sum))
+    sums_img[g_img] = part
     gather(sums_img, send_s1, recv_s1, g_img, img_peers)
     pi = dot(
-        jnp.concatenate([g_hi, g_hi, g_lo, g_lo], axis=0),
-        jnp.concatenate([txt_both, txt_both], axis=0),
+        jnp.concatenate((grads_hi + grads_lo) * 2, axis=0),
+        jnp.concatenate(his * 2 + los * 2, axis=0),
         (0, 0),
     )
     img_part[...] = pi.reshape(n_img, shard, width)
-    scatter(img_part, img_recv, send_pimg, recv_pimg, g_img, img_peers[::-1])
+    scatter(img_part, img_recv, send_pimg, recv_pimg, g_img, img_peers)
 
     drain(sums_img, send_s1, recv_s1, img_peers)
     sums_txt[g_txt] = jnp.sum(sums_img[...], axis=0)
@@ -205,9 +204,7 @@
     drain(sums_txt, send_s2, recv_s2, txt_peers)
     count = float(rows * cols * shard)
     final = jnp.sum(sums_txt[...], axis=0) / count
-    loss, d_temp, d_bias = (total(final[at : at + 8]) for at in (0, 8, 16))
-    lane = lax.broadcasted_iota(jnp.int32, (8, 128), 1)
-    scalars_ref[...] = jnp.where(lane == 0, loss, jnp.where(lane == 1, temp * d_temp, d_bias))
+    scalars_ref[...] = jnp.where(lane == 1, temp * final, final)
 
     sent(txt_part, send_ptxt, recv_ptxt, txt_peers)
     sent(img_part, send_pimg, recv_pimg, img_peers)
@@ -250,7 +247,7 @@
             pltpu.VMEM(block, F32), pltpu.VMEM(block, F32),
             pltpu.VMEM((2 * n_img * shard, width), BF16),
             img_blocks, txt_blocks, img_blocks, txt_blocks, img_blocks, txt_blocks,
-            pltpu.VMEM((n_img, 24, 128), F32), pltpu.VMEM((n_txt, 24, 128), F32),
+            pltpu.VMEM((n_img, 8, 128), F32), pltpu.VMEM((n_txt, 8, 128), F32),
             img_sems, img_sems, txt_sems, txt_sems, img_sems, img_sems, txt_sems, txt_sems,
             img_sems, img_sems, txt_sems, txt_sems, pltpu.SemaphoreType.DMA((2,)),
         ],

time: 23.6 us -> 23.3 us (0.987)
  Pallas kernels: 21.5 us -> 21.2 us
    pallas_call x1, Pallas kernels: 20.8 us -> 20.5 us  [per_device(): pl.pallas_call(functools.partial(kernel, rows, cols, low), out_shape=[plt...]
where the time goes in v4:
time: 23.3 us; the launch traced here: 23.1 us
  Pallas kernels  21.2 us (91%)
  between operations  1.94 us (8%)
    pallas_call x1, Pallas kernels, per_device(): pl.pallas_call(functools.partial(kernel, rows, cols, low), out_shape=[plt...  20.5 us
    pallas_call x1, Pallas kernels, per_device(): pl.pallas_call(write_out, out_shape=[one, one, one, jax.ShapeDtypeStruct(...  0.69 us

profile of v4, /device:TPU:0, one launch (start us, length us, event | category | flops | bytes accessed | tf_op | source)
XLA Modules:
  0.0 23.1 jit_solution(14594743571451329328)
XLA Ops:
  1.9 20.5 %sigmoid_loss.1 = (f32[16,768]{1,0:T(8,128)S(1)}, f32[16,768]{1,0:T(8,128)S(1)}, f32[8,128]{1,0:T(8,128)S(1)}) custom-call(f32[1,128]{1,0:T(1,128)S(1)} %compare_select_fusion.scale_ref, f32[16,768]{1,0:T(8,128)} %images_ref.1, f32[16,768]{1,0:T(8,128)} %texts_ref.1), custom_call_target="tpu_custom_call" | custom-call | tf_op jit(solution)/shard_map/sigmoid_loss/pallas_call | solution.py:237
  22.4 0.7 %write_out.1 = (f32[1,1]{1,0:T(1,128)}, f32[1,1]{1,0:T(1,128)}, f32[1,1]{1,0:T(1,128)}, f32[16,768]{1,0:T(8,128)}, f32[16,768]{1,0:T(8,128)}) custom-call(f32[16,768]{1,0:T(8,128)S(1)} %get-tuple-element.13.grad_img_ref, f32[16,768]{1,0:T(8,128)S(1)} %get-tuple-element.14.grad_txt_ref, f32[8,128]{1,0:T(8,128)S(1)} %get-tuple-element.15.scalars_ref), custom_call_target="tpu_custom_call" | custom-call | tf_op jit(solution)/shard_map/write_out/pallas_call | solution.py:261
  (1 shorter events, 0.0 us)

commit v5 on v4

--- a/solution.py
+++ b/solution.py
@@ -19,17 +19,6 @@
 
 def dot(a, b, contract):
     return lax.dot_general(a, b, ((contract[:1], contract[1:]), ((), ())), preferred_element_type=F32)
-
-
-def paired(slot, step, count):
-    if count & (count - 1):
-        return lax.rem(slot + step, count)
-    bit = 1
-    while bit < count:
-        if step & bit:
-            slot = slot + bit - 2 * bit * lax.rem(lax.div(slot, bit), 2)
-        bit *= 2
-    return slot
 
 
 def normalize(x):
@@ -67,14 +56,19 @@
 
     img_peers, txt_peers = [], []
     for step in range(1, n_txt):
-        slot = paired(g_txt, step, n_txt)
+        slot = lax.rem(g_txt + step, n_txt)
         txt_peers.append((slot, (slot * low + below, col)))
     def img_device(slot):
         return high * low + lax.div(slot, cols), lax.rem(slot, cols)
 
+    def sibling(slot):
+        return slot + 1 - 2 * lax.rem(slot, 2)
+
     for step in range(1, n_img):
-        slot = 2 * paired(lax.div(g_img, 2), step // 2, n_img // 2) + lax.rem(g_img + step, 2)
+        slot = 2 * lax.rem(lax.div(g_img, 2) + step // 2, n_img // 2) + lax.rem(g_img + step, 2)
         img_peers.append((slot, img_device(slot)))
+    same_core, other_core = img_peers[1::2], img_peers[0::2]
+    twin = other_core[0]
 
     barrier = pltpu.get_barrier_semaphore()
     for _, peer in txt_peers + img_peers:
@@ -121,10 +115,14 @@
             copy(src.at[slot], src.at[slot], send.at[slot], recv.at[slot], peer).wait_send()
 
     gather(txt_all, send_txt, recv_txt, g_txt, txt_peers)
-    gather(img_all, send_img, recv_img, g_img, img_peers)
+    gather(img_all, send_img, recv_img, g_img, [twin] + same_core)
 
     keep(img_both, g_img, m_img, unit_img)
-    for slot, peer in img_peers:
+    for slot, peer in same_core:
+        arrive(img_all, send_img, recv_img, slot, peer)
+        copy(img_all.at[slot], img_all.at[slot], send_img.at[sibling(slot)], recv_img.at[slot], twin[1]).start()
+        keep(img_both, slot, m_img, img_all[slot])
+    for slot, peer in other_core:
         arrive(img_all, send_img, recv_img, slot, peer)
         keep(img_both, slot, m_img, img_all[slot])
 

time: 23.3 us -> 22.8 us (0.979)
  Pallas kernels: 21.2 us -> 20.7 us
    pallas_call x1, Pallas kernels: 20.5 us -> 20 us  [per_device(): pl.pallas_call(functools.partial(kernel, rows, cols, low), out_shape=[plt...]
where the time goes in v5:
time: 22.8 us; the launch traced here: 22.6 us
  Pallas kernels  20.7 us (91%)
  between operations  1.94 us (9%)
    pallas_call x1, Pallas kernels, per_device(): pl.pallas_call(functools.partial(kernel, rows, cols, low), out_shape=[plt...  20 us
    pallas_call x1, Pallas kernels, per_device(): pl.pallas_call(write_out, out_shape=[one, one, one, jax.ShapeDtypeStruct(...  0.69 us

profile of v5, /device:TPU:0, one launch (start us, length us, event | category | flops | bytes accessed | tf_op | source)
XLA Modules:
  0.0 22.6 jit_solution(7845146450432468838)
XLA Ops:
  1.9 20.0 %sigmoid_loss.1 = (f32[16,768]{1,0:T(8,128)S(1)}, f32[16,768]{1,0:T(8,128)S(1)}, f32[8,128]{1,0:T(8,128)S(1)}) custom-call(f32[1,128]{1,0:T(1,128)S(1)} %compare_select_fusion.scale_ref, f32[16,768]{1,0:T(8,128)} %images_ref.1, f32[16,768]{1,0:T(8,128)} %texts_ref.1), custom_call_target="tpu_custom_call" | custom-call | tf_op jit(solution)/shard_map/sigmoid_loss/pallas_call | solution.py:235
  21.9 0.7 %write_out.1 = (f32[1,1]{1,0:T(1,128)}, f32[1,1]{1,0:T(1,128)}, f32[1,1]{1,0:T(1,128)}, f32[16,768]{1,0:T(8,128)}, f32[16,768]{1,0:T(8,128)}) custom-call(f32[16,768]{1,0:T(8,128)S(1)} %get-tuple-element.13.grad_img_ref, f32[16,768]{1,0:T(8,128)S(1)} %get-tuple-element.14.grad_txt_ref, f32[8,128]{1,0:T(8,128)S(1)} %get-tuple-element.15.scalars_ref), custom_call_target="tpu_custom_call" | custom-call | tf_op jit(solution)/shard_map/write_out/pallas_call | solution.py:259
  (1 shorter events, 0.0 us)

commit v6 on v2

--- a/solution.py
+++ b/solution.py
@@ -58,9 +58,17 @@
     for step in range(1, n_txt):
         slot = lax.rem(g_txt + step, n_txt)
         txt_peers.append((slot, (slot * low + below, col)))
+    def img_device(slot):
+        return high * low + lax.div(slot, cols), lax.rem(slot, cols)
+
+    def sibling(slot):
+        return slot + 1 - 2 * lax.rem(slot, 2)
+
     for step in range(1, n_img):
-        slot = lax.rem(g_img + step, n_img)
-        img_peers.append((slot, (high * low + lax.div(slot, cols), lax.rem(slot, cols))))
+        slot = 2 * lax.rem(lax.div(g_img, 2) + step // 2, n_img // 2) + lax.rem(g_img + step, 2)
+        img_peers.append((slot, img_device(slot)))
+    same_core, other_core = img_peers[1::2], img_peers[0::2]
+    twin = other_core[0]
 
     barrier = pltpu.get_barrier_semaphore()
     for _, peer in txt_peers + img_peers:
@@ -107,13 +115,17 @@
             copy(src.at[slot], src.at[slot], send.at[slot], recv.at[slot], peer).wait_send()
 
     gather(txt_all, send_txt, recv_txt, g_txt, txt_peers)
-    gather(img_all, send_img, recv_img, g_img, img_peers)
+    gather(img_all, send_img, recv_img, g_img, [twin] + same_core)
 
     keep(txt_both, g_txt, m_txt, unit_txt)
     keep(img_both, g_img, m_img, unit_img)
     temp = jnp.exp(jnp.full((1, 1), log_temp_ref[0], F32))
     shift = bias_ref[0]
-    for slot, peer in img_peers:
+    for slot, peer in same_core:
+        arrive(img_all, send_img, recv_img, slot, peer)
+        copy(img_all.at[slot], img_all.at[slot], send_img.at[sibling(slot)], recv_img.at[slot], twin[1]).start()
+        keep(img_both, slot, m_img, img_all[slot])
+    for slot, peer in other_core:
         arrive(img_all, send_img, recv_img, slot, peer)
         keep(img_both, slot, m_img, img_all[slot])
     for slot, peer in txt_peers:

time: 22.5 us -> 22.5 us (level)
  no operation moved by 1% of the time
where the time goes in v6:
time: 22.5 us; the launch traced here: 22.3 us
  Pallas kernels  20.4 us (91%)
  between operations  1.93 us (9%)
    pallas_call x1, Pallas kernels, per_device(): pl.pallas_call(functools.partial(kernel, rows, cols, low), out_shape=[plt...  19.7 us
    pallas_call x1, Pallas kernels, per_device(): pl.pallas_call(write_out, out_shape=[one, one, one, jax.ShapeDtypeStruct(...  0.69 us

profile of v6, /device:TPU:0, one launch (start us, length us, event | category | flops | bytes accessed | tf_op | source)
XLA Modules:
  0.0 22.3 jit_solution(5386170317563676315)
XLA Ops:
  1.9 19.7 %sigmoid_loss.1 = (f32[16,768]{1,0:T(8,128)S(1)}, f32[16,768]{1,0:T(8,128)S(1)}, f32[8,128]{1,0:T(8,128)S(1)}) custom-call(f32[1]{0:T(128)S(6)} %copy.9.log_temp_ref, f32[1]{0:T(128)S(6)} %copy.10.bias_ref, f32[16,768]{1,0:T(8,128)} %images_ref.1, f32[16,768]{1,0:T(8,128)} %texts_ref.1), custom_call_target="tpu_custom_call" | custom-call | tf_op jit(solution)/shard_map/sigmoid_loss/pallas_call | solution.py:219
  21.6 0.7 %write_out.1 = (f32[1,1]{1,0:T(1,128)}, f32[1,1]{1,0:T(1,128)}, f32[1,1]{1,0:T(1,128)}, f32[16,768]{1,0:T(8,128)}, f32[16,768]{1,0:T(8,128)}) custom-call(f32[16,768]{1,0:T(8,128)S(1)} %get-tuple-element.13.grad_img_ref, f32[16,768]{1,0:T(8,128)S(1)} %get-tuple-element.14.grad_txt_ref, f32[8,128]{1,0:T(8,128)S(1)} %get-tuple-element.15.scalars_ref), custom_call_target="tpu_custom_call" | custom-call | tf_op jit(solution)/shard_map/write_out/pallas_call | solution.py:243
